TPU v7x, 512 devices: a whole 4x8x8 slice. The times are simulated.
512 devices in a mesh: ctx: 32 (over x, z), head: 16 (over y, core).
Axes of the slice: x: 4, y: 8, z: 8, core: 2. Of those that a mesh axis runs over, the one named last changes fastest.
Arguments:
- features: float32 [8192, 8192], P(('ctx', 'head')), may hold values from -6 to 6
- write_proj: float32 [8192, 512], P(('ctx', 'head')), may hold values from -2.5 to 2.5
- read_proj: float32 [8192, 512], P(('ctx', 'head')), may hold values from -2.5 to 2.5
- step_size: float32 [8192, 128], P(('ctx', 'head')), as said below
- decay_rate: float32 [128], P('head'), as said below
- skip_weight: float32 [128], P('head'), may hold values from 0.5 to 1.5
- upstream: float32 [8192, 8192], P(('ctx', 'head')), may hold values from -6 to 6
Outputs:
- features_grad: float32 [8192, 8192], P(('ctx', 'head'))
- write_grad: float32 [8192, 512], P(('ctx', 'head'))
- read_grad: float32 [8192, 512], P(('ctx', 'head'))
- step_grad: float32 [8192, 128], P(('ctx', 'head'))
Inputs may be any that keep to these rules, and one draw needn't show every extreme that they name: `step_size`: every entry is positive. `decay_rate`: every entry is positive.
All inputs are finite; a program needn't handle non-finite values.
Results may differ from a plain program's by a relative error of at most 0.00018.
Values sent between devices are 32-bit elements; how exact they have to be, the bound alone decides.
A program may use at most 64 MiB of HBM per device.

v0:
```python
import jax
import jax.numpy as jnp
from jax import lax
from jax.sharding import PartitionSpec as P

STATE = 128
GROUPS = 4
BLOCK = 128


def entering_2(part, axis, combine, identity, reverse):
    count = lax.axis_size(axis)
    place = lax.axis_index(axis)
    ahead = count - 1 - place if reverse else place
    gathered = jax.tree.map(lambda a: lax.all_gather(a, axis), part)
    state = jax.tree.map(lambda a, e: jnp.zeros_like(a) + jnp.asarray(e, a.dtype), part, identity)

    def one(lap, state):
        source = count - 1 - lap if reverse else lap
        return combine(
            state, jax.tree.map(lambda a: lax.dynamic_index_in_dim(a, source, 0, False), gathered)
        )

    return lax.fori_loop(0, ahead, one, state)


def forward_combine(earlier, later):
    return (earlier[0] * later[0], later[0][:, None, None] * earlier[1] + later[1])


def backward_combine(earlier, later):
    return (earlier[0] * later[0], later[1] + later[0][:, None, None] * earlier[1])


def on_device(features, write_proj, read_proj, step_size, decay_rate, skip_weight, upstream):
    high = lax.Precision.HIGHEST
    devices = lax.axis_size("head")
    local_tok = features.shape[0]
    heads_all = step_size.shape[1]
    head_local = heads_all // devices
    width = features.shape[1] // heads_all
    per_group = heads_all // GROUPS
    copies_count = max(1, per_group // head_local)
    group_local = max(1, head_local // per_group)
    heads_per_local = head_local // group_local
    feats, grads_in, steps = (
        lax.all_to_all(features, "head", split_axis=1, concat_axis=0, tiled=True),
        lax.all_to_all(upstream, "head", split_axis=1, concat_axis=0, tiled=True),
        lax.all_to_all(step_size, "head", split_axis=1, concat_axis=0, tiled=True),
    )
    whole_write, whole_read = (
        lax.all_gather(write_proj, "head", axis=0, tiled=True),
        lax.all_gather(read_proj, "head", axis=0, tiled=True),
    )
    first = lax.axis_index("head") * head_local // per_group
    total_rows = whole_write.shape[0]
    writes = lax.dynamic_slice_in_dim(
        whole_write.reshape(total_rows, GROUPS, STATE), first, group_local, 1
    ).reshape(total_rows, group_local * STATE)
    reads = lax.dynamic_slice_in_dim(
        whole_read.reshape(total_rows, GROUPS, STATE), first, group_local, 1
    ).reshape(total_rows, group_local * STATE)
    rows_all = feats.shape[0]
    blocks = rows_all // BLOCK
    feat = feats.reshape(blocks, BLOCK, head_local, width)
    grad_y = grads_in.reshape(blocks, BLOCK, head_local, width)
    step = steps.reshape(blocks, BLOCK, head_local)
    write_group = writes.reshape(blocks, BLOCK, group_local, STATE)
    read_group = reads.reshape(blocks, BLOCK, group_local, STATE)
    write_heads = jnp.repeat(write_group, heads_per_local, axis=2)
    read_heads = jnp.repeat(read_group, heads_per_local, axis=2)
    positions = jnp.arange(BLOCK)
    lower = positions[:, None] >= positions[None, :]
    lower_f = lower.astype(jnp.float32)
    log_step = -step * decay_rate[None, None, :]
    cumul = jnp.einsum("ij,bjh->bih", lower_f, log_step, precision=high)
    across = jnp.swapaxes(cumul, 1, 2)
    gaps = across[:, :, :, None] - across[:, :, None, :]
    decays = jnp.where(lower, jnp.exp(jnp.where(lower, gaps, 0.0)), 0.0)
    scores_group = jnp.einsum("bign,bjgn->bgij", read_group, write_group, precision=high)
    scores = jnp.repeat(scores_group, heads_per_local, axis=1)
    mixing = scores * decays
    scaled = step[..., None] * feat
    tail = jnp.exp(cumul[:, -1, :])
    weights = jnp.exp(cumul[:, -1:, :] - cumul)
    growth = jnp.exp(cumul)
    local_state = jnp.einsum(
        "bjhn,bjhp->bhnp", write_heads * weights[..., None], scaled, precision=high
    )
    local_grad = jnp.einsum(
        "bihn,bihp->bhnp", read_heads * growth[..., None], grad_y, precision=high
    )
    dev_decay = jnp.ones((head_local,), jnp.float32)
    dev_state = jnp.zeros((head_local, STATE, width), jnp.float32)
    dev_grad = jnp.zeros((head_local, STATE, width), jnp.float32)
    for index in range(blocks):
        dev_state = tail[index][:, None, None] * dev_state + local_state[index]
        dev_decay = dev_decay * tail[index]
    for index in reversed(range(blocks)):
        dev_grad = local_grad[index] + tail[index][:, None, None] * dev_grad
    identity = (
        jnp.ones((head_local,), jnp.float32),
        jnp.zeros((head_local, STATE, width), jnp.float32),
    )
    entering = entering_2((dev_decay, dev_state), "ctx", forward_combine, identity, False)[1]
    leaving = entering_2((dev_decay, dev_grad), "ctx", backward_combine, identity, True)[1]
    starts = []
    carried = entering
    for index in range(blocks):
        starts.append(carried)
        carried = tail[index][:, None, None] * carried + local_state[index]
    finals = [carried] * blocks
    carried = leaving
    for index in reversed(range(blocks)):
        finals[index] = carried
        carried = local_grad[index] + tail[index][:, None, None] * carried
    start_states = jnp.stack(starts)
    end_grads = jnp.stack(finals)
    outer_y = growth[..., None] * jnp.einsum(
        "bihn,bhnp->bihp", read_heads, start_states, precision=high
    )
    pass_back = jnp.einsum("bjhn,bhnp->bjhp", write_heads, end_grads, precision=high)
    grad_scaled = (
        jnp.einsum("bhij,bihp->bjhp", mixing, grad_y, precision=high)
        + weights[..., None] * pass_back
    )
    grad_feat = step[..., None] * grad_scaled + skip_weight[None, None, :, None] * grad_y
    grad_mix = jnp.einsum("bihp,bjhp->bhij", grad_y, scaled, precision=high) * lower_f
    grad_scores = (
        (grad_mix * decays).reshape(blocks, group_local, heads_per_local, BLOCK, BLOCK).sum(axis=2)
    )
    read_extra = growth[..., None] * jnp.einsum(
        "bhnp,bihp->bihn", start_states, grad_y, precision=high
    )
    write_extra = weights[..., None] * jnp.einsum(
        "bhnp,bjhp->bjhn", end_grads, scaled, precision=high
    )
    grad_read = jnp.einsum("bgij,bjgn->bign", grad_scores, write_group, precision=high)
    grad_read = grad_read + read_extra.reshape(
        blocks, BLOCK, group_local, heads_per_local, STATE
    ).sum(axis=3)
    grad_write = jnp.einsum("bgij,bign->bjgn", grad_scores, read_group, precision=high)
    grad_write = grad_write + write_extra.reshape(
        blocks, BLOCK, group_local, heads_per_local, STATE
    ).sum(axis=3)
    product = grad_mix * mixing
    grad_cum = jnp.swapaxes(product.sum(axis=3) - product.sum(axis=2), 1, 2)
    grad_cum = grad_cum + jnp.sum(grad_y * outer_y, axis=3)
    along = jnp.sum(scaled * pass_back, axis=3)
    grad_cum = grad_cum - weights * along
    last_term = tail * jnp.sum(end_grads * start_states, axis=(2, 3)) + jnp.sum(
        weights * along, axis=1
    )
    last_row = (positions == BLOCK - 1).astype(jnp.float32)
    grad_cum = grad_cum + last_row[None, :, None] * last_term[:, None, :]
    grad_log = jnp.einsum("ik,bih->bkh", lower_f, grad_cum, precision=high)
    grad_step = jnp.sum(feat * grad_scaled, axis=3) - decay_rate[None, None, :] * grad_log
    back_feat, back_step, back_write, back_read = (
        lax.all_to_all(
            grad_feat.reshape(rows_all, head_local * width),
            "head",
            split_axis=0,
            concat_axis=1,
            tiled=True,
        ),
        lax.all_to_all(
            grad_step.reshape(rows_all, head_local), "head", split_axis=0, concat_axis=1, tiled=True
        ),
        lax.all_to_all(
            grad_write.reshape(rows_all, group_local * STATE),
            "head",
            split_axis=0,
            concat_axis=1,
            tiled=True,
        ),
        lax.all_to_all(
            grad_read.reshape(rows_all, group_local * STATE),
            "head",
            split_axis=0,
            concat_axis=1,
            tiled=True,
        ),
    )

    def fold_pairs(matrix):
        return (
            matrix.reshape(local_tok, GROUPS, copies_count, STATE)
            .sum(axis=2)
            .reshape(local_tok, GROUPS * STATE)
        )

    return (back_feat, fold_pairs(back_write), fold_pairs(back_read), back_step)


def solution(mesh):
    placed = (
        P(("ctx", "head"), None),
        P(("ctx", "head"), None),
        P(("ctx", "head"), None),
        P(("ctx", "head"), None),
        P("head"),
        P("head"),
        P(("ctx", "head"), None),
    )
    return jax.shard_map(
        on_device,
        mesh=mesh,
        in_specs=placed,
        out_specs=(
            P(("ctx", "head"), None),
            P(("ctx", "head"), None),
            P(("ctx", "head"), None),
            P(("ctx", "head"), None),
        ),
        check_vma=False,
    )
```

profile of v0, /device:TPU:1, one launch (start us, length us, event | category | flops | bytes accessed | tf_op | source)
XLA Modules:
  0.0 416.9 jit_solution(14270278716696811555)
XLA Ops:
  8.7 10.1 %all-to-all-start = ((f32[16,1,128]{2,1,0:T(1,128)}), f32[16,1,128]{2,1,0:T(1,128)S(1)}, u32[]{:S(2)}, u32[]{:S(2)}) async-start(f32[16,1,128]{2,1,0:T(1,128)} %reshape.175), calls=%async_computation | async-start | bytes 16384 | tf_op jit(solution)/shard_map/all_to_all | solution.py:49
  18.9 18.9 %all_gather.21 = f32[256,512]{1,0:T(8,128)S(1)} all-gather(f32[16,512]{1,0:T(8,128)} %param.12), channel_id=1, replica_groups=mesh['ctx'=32,'head'=16] {'head'}, dimensions={0}, use_global_device_ids=true | all-gather | bytes 557056 | tf_op jit(solution)/shard_map/all_gather | solution.py:52
  38.1 1.9 copy.241
  40.0 4.7 %all-to-all-start.3 = ((f32[16,16,512]{2,0,1:T(8,128)}), f32[16,16,512]{2,0,1:T(8,128)S(1)}, u32[]{:S(2)}, u32[]{:S(2)}) async-start(f32[16,16,512]{2,0,1:T(8,128)} %bitcast.174), calls=%async_computation.3 | async-start | bytes 1048576 | tf_op jit(solution)/shard_map/all_to_all | solution.py:47
  48.4 13.6 %all-to-all-done.3 = f32[16,16,512]{2,0,1:T(8,128)S(1)} async-done(((f32[16,16,512]{2,0,1:T(8,128)}), f32[16,16,512]{2,0,1:T(8,128)S(1)}, u32[]{:S(2)}, u32[]{:S(2)}) %all-to-all-start.3) | async-done | bytes 524320 | tf_op jit(solution)/shard_map/all_to_all | solution.py:47
  65.5 3.5 all-to-all-start.1
  69.1 26.7 %all_gather.20 = f32[256,512]{1,0:T(8,128)S(1)} all-gather(f32[16,512]{1,0:T(8,128)S(1)} %copy-done.10), channel_id=1, replica_groups=mesh['ctx'=32,'head'=16] {'head'}, dimensions={0}, use_global_device_ids=true | all-gather | bytes 557056 | tf_op jit(solution)/shard_map/all_gather | solution.py:53
  96.7 2.1 fusion.15
  101.5 39.2 %all-gather = f32[32,1,8]{2,1,0:T(1,128)} all-gather(f32[1,1,8]{2,1,0:T(1,128)} %get-tuple-element.245), channel_id=1, replica_groups=mesh['ctx'=32,'head'=16] {'ctx'}, dimensions={0}, use_global_device_ids=true | all-gather | bytes 1056 | tf_op jit(solution)/shard_map/all_gather | solution.py:15
  140.7 3.7 fusion.20
  144.4 22.8 %all-gather.6.cloned.1.call-done = f32[32,8,128,64]{2,3,1,0:T(8,128)} async-done(((f32[1,8,128,64]{2,3,1,0:T(8,128)}), f32[32,8,128,64]{2,3,1,0:T(8,128)}) %all-gather.6.cloned.1.call-update) | async-done | bytes 8388624 | tf_op jit(solution)/shard_map/all_gather | solution.py:15
  168.1 103.8 %all-gather.4.cloned.1.call-done = f32[32,8,128,64]{2,3,1,0:T(8,128)} async-done(((f32[1,8,128,64]{2,3,1,0:T(8,128)}), f32[32,8,128,64]{2,3,1,0:T(8,128)}) %all-gather.4.cloned.1.call-update) | async-done | bytes 8388624 | tf_op jit(solution)/shard_map/all_gather | solution.py:15
  272.0 63.7 %while.26 = (s32[]{:T(128)}, f32[8,128,64]{2,1,0:T(8,128)S(1)}, s32[]{:T(128)}, f32[32,8,128,64]{2,3,1,0:T(8,128)}, f32[32,8]{1,0:T(8,128)}, /*index=5*/s32[]{:T(128)}, s32[]{:T(128)}, s32[]{:T(128)}, s32[]{:T(128)}) while((s32[]{:T(128)}, f32[8,128,64]{2,1,0:T(8,128)S(1)}, s32[]{:T(128)}, f32[32,8,128,64]{2,3,1,0:T(8,128)}, ...), condition=%wide.region_1.2_spmd, body=%wide.region_0.1_spmd.sunk | while | flops 131078 | bytes 1835251 | solution.py:24
  336.6 2.1 convolution_bitcast_fusion.4
  342.6 3.2 multiply_reduce_fusion.2
  348.7 7.8 %all-to-all-start.6 = ((f32[16,1,128]{2,1,0:T(1,128)}), f32[16,1,128]{2,1,0:T(1,128)S(1)}, u32[]{:S(2)}, u32[]{:S(2)}) async-start(f32[16,1,128]{2,1,0:T(1,128)} %reshape.177), calls=%async_computation.6 | async-start | bytes 16384 | tf_op jit(solution)/shard_map/all_to_all | solution.py:166
  357.7 5.8 %all-to-all-done.6 = f32[16,1,128]{2,1,0:T(1,128)S(1)} async-done(((f32[16,1,128]{2,1,0:T(1,128)}), f32[16,1,128]{2,1,0:T(1,128)S(1)}, u32[]{:S(2)}, u32[]{:S(2)}) %all-to-all-start.6) | async-done | bytes 8224 | tf_op jit(solution)/shard_map/all_to_all | solution.py:166
  363.5 4.0 all-to-all-start.5
  367.4 2.0 fusion.3
  370.4 6.3 %all-to-all-done.5 = f32[16,16,128]{2,1,0:T(8,128)S(1)} async-done(((f32[16,16,128]{2,1,0:T(8,128)}), f32[16,16,128]{2,1,0:T(8,128)S(1)}, u32[]{:S(2)}, u32[]{:S(2)}) %all-to-all-start.5) | async-done | bytes 131104 | tf_op jit(solution)/shard_map/all_to_all | solution.py:176
  376.6 3.4 all-to-all-start.4
  381.5 7.0 %all-to-all-done.4 = f32[16,16,128]{2,1,0:T(8,128)S(1)} async-done(((f32[16,16,128]{2,1,0:T(8,128)}), f32[16,16,128]{2,1,0:T(8,128)S(1)}, u32[]{:S(2)}, u32[]{:S(2)}) %all-to-all-start.4) | async-done | bytes 131104 | tf_op jit(solution)/shard_map/all_to_all | solution.py:169
  388.6 3.5 all-to-all-start.2
  394.7 14.5 %all-to-all-done.2 = f32[16,16,512]{2,1,0:T(8,128)S(1)} async-done(((f32[16,16,512]{2,1,0:T(8,128)}), f32[16,16,512]{2,1,0:T(8,128)S(1)}, u32[]{:S(2)}, u32[]{:S(2)}) %all-to-all-start.2) | async-done | bytes 524320 | tf_op jit(solution)/shard_map/all_to_all | solution.py:159
  (226 shorter events, 90.4 us)
Async XLA Ops:
  7.2 57.5 %copy-start.3 = (f32[16,8192]{1,0:T(8,128)S(1)}, f32[16,8192]{1,0:T(8,128)}, u32[]{:S(2)}) copy-start(f32[16,8192]{1,0:T(8,128)} %param.17) | copy-start | bytes 1572868
  7.2 61.9 %copy-start.10 = (f32[16,512]{1,0:T(8,128)S(1)}, f32[16,512]{1,0:T(8,128)}, u32[]{:S(2)}) copy-start(f32[16,512]{1,0:T(8,128)} %param.13) | copy-start | bytes 98308
  8.7 31.3 %all-to-all-start = ((f32[16,1,128]{2,1,0:T(1,128)}), f32[16,1,128]{2,1,0:T(1,128)S(1)}, u32[]{:S(2)}, u32[]{:S(2)}) async-start(f32[16,1,128]{2,1,0:T(1,128)} %reshape.175), calls=%async_computation | async-start | bytes 16384 | tf_op jit(solution)/shard_map/all_to_all | solution.py:49
  40.0 22.0 %all-to-all-start.3 = ((f32[16,16,512]{2,0,1:T(8,128)}), f32[16,16,512]{2,0,1:T(8,128)S(1)}, u32[]{:S(2)}, u32[]{:S(2)}) async-start(f32[16,16,512]{2,0,1:T(8,128)} %bitcast.174), calls=%async_computation.3 | async-start | bytes 1048576 | tf_op jit(solution)/shard_map/all_to_all | solution.py:47
  44.7 122.5 %all-gather.6.cloned.1.call-start = ((), (), s32[]{:S(2)}) async-start(), calls=%async_computation.8 | async-start | bytes 8650752 | tf_op jit(solution)/shard_map/all_gather | solution.py:15
  46.2 22.8 %copy-start.8 = (f32[2,128,8]{1,2,0:T(8,128)}, f32[2,128,8]{1,2,0:T(8,128)S(1)}, u32[]{:S(2)}) copy-start(f32[2,128,8]{1,2,0:T(8,128)S(1)} %copy.180) | copy-start | bytes 24580
  47.2 21.8 %copy-start.11 = (f32[2,8]{1,0:T(2,128)}, f32[2,8]{1,0:T(2,128)S(1)}, u32[]{:S(2)}) copy-start(f32[2,8]{1,0:T(2,128)S(1)} %slice_reduce_fusion) | copy-start | bytes 196
  47.8 21.2 %copy-start.13 = (f32[8]{0:T(128)}, f32[8]{0:T(128)S(1)}, u32[]{:S(2)}) copy-start(f32[8]{0:T(128)S(1)} %get-tuple-element.244) | copy-start | bytes 100
  48.4 20.6 %copy-start.6 = (f32[2,128,8]{1,2,0:T(8,128)}, f32[2,128,8]{1,2,0:T(8,128)S(1)}, u32[]{:S(2)}) copy-start(f32[2,128,8]{1,2,0:T(8,128)S(1)} %get-tuple-element.240) | copy-start | bytes 24580
  65.5 30.7 %all-to-all-start.1 = ((f32[16,16,512]{2,0,1:T(8,128)}), f32[16,16,512]{2,0,1:T(8,128)S(1)}, u32[]{:S(2)}, u32[]{:S(2)}) async-start(f32[16,16,512]{2,0,1:T(8,128)} %bitcast.175), calls=%async_computation.1 | async-start | bytes 1048576 | tf_op jit(solution)/shard_map/all_to_all | solution.py:48
  69.0 203.0 %all-gather.4.cloned.1.call-start = ((), (), s32[]{:S(2)}) async-start(), calls=%async_computation.7 | async-start | bytes 8650752 | tf_op jit(solution)/shard_map/all_gather | solution.py:15
  96.0 71.2 %copy-start = (f32[256,1,128]{2,1,0:T(1,128)}, f32[256,1,128]{2,1,0:T(1,128)S(1)}, u32[]{:S(2)}) copy-start(f32[256,1,128]{2,1,0:T(1,128)S(1)} %constant_dynamic-slice_fusion.3) | copy-start | bytes 393220
  96.1 71.1 %copy-start.2 = (f32[2,128,128]{1,2,0:T(8,128)}, f32[2,128,128]{1,2,0:T(8,128)S(1)}, u32[]{:S(2)}) copy-start(f32[2,128,128]{1,2,0:T(8,128)S(1)} %copy.189) | copy-start | bytes 393220
  100.4 66.8 %copy-start.12 = (pred[128,128]{0,1:T(8,128)(4,1)}, pred[128,128]{0,1:T(8,128)(4,1)S(1)}, u32[]{:S(2)}) copy-start(pred[128,128]{0,1:T(8,128)(4,1)S(1)} %copy.184) | copy-start | bytes 49156
  101.5 65.7 %copy-start.5 = (f32[2,128,128]{1,2,0:T(8,128)}, f32[2,128,128]{1,2,0:T(8,128)S(1)}, u32[]{:S(2)}) copy-start(f32[2,128,128]{1,2,0:T(8,128)S(1)} %fusion.63) | copy-start | bytes 393220
  335.6 33.8 %copy-start.1 = (f32[256,1,128]{2,1,0:T(1,128)S(1)}, f32[256,1,128]{2,1,0:T(1,128)}, u32[]{:S(2)}) copy-start(f32[256,1,128]{2,1,0:T(1,128)} %copy-done) | copy-start | bytes 393220
  336.5 20.1 %copy-start.4 = (f32[2,128,128]{1,2,0:T(8,128)S(1)}, f32[2,128,128]{1,2,0:T(8,128)}, u32[]{:S(2)}) copy-start(f32[2,128,128]{1,2,0:T(8,128)} %get-tuple-element.216) | copy-start | bytes 393220
  336.6 30.9 %copy-start.7 = (f32[2,128,8]{1,2,0:T(8,128)S(1)}, f32[2,128,8]{1,2,0:T(8,128)}, u32[]{:S(2)}) copy-start(f32[2,128,8]{1,2,0:T(8,128)} %copy-done.6) | copy-start | bytes 24580
  336.6 30.9 %copy-start.9 = (f32[2,128,8]{1,2,0:T(8,128)S(1)}, f32[2,128,8]{1,2,0:T(8,128)}, u32[]{:S(2)}) copy-start(f32[2,128,8]{1,2,0:T(8,128)} %copy-done.8) | copy-start | bytes 24580
  348.7 14.8 %all-to-all-start.6 = ((f32[16,1,128]{2,1,0:T(1,128)}), f32[16,1,128]{2,1,0:T(1,128)S(1)}, u32[]{:S(2)}, u32[]{:S(2)}) async-start(f32[16,1,128]{2,1,0:T(1,128)} %reshape.177), calls=%async_computation.6 | async-start | bytes 16384 | tf_op jit(solution)/shard_map/all_to_all | solution.py:166
  363.5 13.2 %all-to-all-start.5 = ((f32[16,16,128]{2,1,0:T(8,128)}), f32[16,16,128]{2,1,0:T(8,128)S(1)}, u32[]{:S(2)}, u32[]{:S(2)}) async-start(f32[16,16,128]{2,1,0:T(8,128)} %bitcast.37), calls=%async_computation.5 | async-start | bytes 262144 | tf_op jit(solution)/shard_map/all_to_all | solution.py:176
  376.6 11.9 %all-to-all-start.4 = ((f32[16,16,128]{2,1,0:T(8,128)}), f32[16,16,128]{2,1,0:T(8,128)S(1)}, u32[]{:S(2)}, u32[]{:S(2)}) async-start(f32[16,16,128]{2,1,0:T(8,128)} %bitcast.27), calls=%async_computation.4 | async-start | bytes 262144 | tf_op jit(solution)/shard_map/all_to_all | solution.py:169
  388.6 20.7 %all-to-all-start.2 = ((f32[16,16,512]{2,1,0:T(8,128)}), f32[16,16,512]{2,1,0:T(8,128)S(1)}, u32[]{:S(2)}, u32[]{:S(2)}) async-start(f32[16,16,512]{2,1,0:T(8,128)} %all_to_all.94), calls=%async_computation.2 | async-start | bytes 1048576 | tf_op jit(solution)/shard_map/all_to_all | solution.py:159
Sparse Core Ops, SparseCore 0:
  64.7 102.3 all-gather.5
  170.9 100.9 all-gather.3
where the time goes:
time: 420 us; the launch traced here: 417 us
  waiting for transfers between devices  174 us (41%)
  blocking collectives  84.7 us (20%)
  local copies, waits for them, and re-layouts  70.8 us (17%)
  starting transfers between devices  37 us (9%)
  matrix products  22.1 us (5%)
  between operations  14.6 us (3%)
  other arithmetic  12.4 us (3%)
    all_gather x2, waiting for transfers between devices, entering_2(): gathered = jax.tree.map(lambda a: lax.all_gather(a, axis), part)  127 us
    all_gather x1, blocking collectives, entering_2(): gathered = jax.tree.map(lambda a: lax.all_gather(a, axis), part)  39.2 us
    dynamic_slice x62, local copies, waits for them, and re-layouts, one(): lax.dynamic_index_in_dim(a, source, 0, False)  36.4 us
    all_gather x1, blocking collectives, on_device(): lax.all_gather(read_proj, 'head', axis=0, tiled=True)  26.7 us
    mul x31, local copies, waits for them, and re-layouts, backward_combine(): later[0][:, None, None] * earlier[1]  21.3 us
    all_gather x1, blocking collectives, on_device(): lax.all_gather(write_proj, 'head', axis=0, tiled=True)  18.9 us
    all_to_all x1, waiting for transfers between devices, on_device(): lax.all_to_all(grad_feat.reshape(rows_all, head_local * width), 'head', s...  14.5 us
    all_to_all x1, waiting for transfers between devices, on_device(): lax.all_to_all(features, 'head', split_axis=1, concat_axis=0, tiled=True)  13.6 us
  transfers between devices with their start and end apart: 9, of which 7 were waited for; matrix products, arithmetic and copies ran while one was open for 6% of the time, Pallas kernels for 0%

commit v1 on v0

v1 whole, which is shorter than its diff:
```python
import functools

import jax
import jax.numpy as jnp
from jax import lax
from jax.experimental import pallas as pl
from jax.experimental.pallas import tpu as pltpu
from jax.sharding import PartitionSpec as P

STATE = 128
GROUPS = 4
WIDTH = 64
MESH = pl.DeviceIdType.MESH
F32 = jnp.float32
HIGH = lax.Precision.HIGH


def mm(a, b, dims, precision=HIGH):
    return lax.dot_general(
        a, b, (dims, ((), ())), precision=precision, preferred_element_type=F32
    )


def nn(a, b, precision=HIGH):
    return mm(a, b, ((1,), (0,)), precision)


def nt(a, b, precision=HIGH):
    return mm(a, b, ((1,), (1,)), precision)


def tn(a, b, precision=HIGH):
    return mm(a, b, ((0,), (0,)), precision)


def parts_of(a, count):
    out = []
    for _ in range(count):
        piece = a.astype(jnp.bfloat16)
        out.append(piece)
        a = a - piece.astype(F32)
    return out


def exact_nn(a, ones):
    n = a.shape[0]
    stacked = jnp.concatenate([p.astype(F32) for p in parts_of(a, 3)], axis=0)
    out = nn(stacked.astype(jnp.bfloat16), ones.astype(jnp.bfloat16), None)
    return (out[2 * n :] + out[n : 2 * n]) + out[:n]


def exact_tn(a, ones):
    stacked = jnp.concatenate([p.astype(F32) for p in parts_of(a, 3)][::-1], axis=0)
    tall = jnp.concatenate([ones] * 3, axis=0)
    return tn(stacked.astype(jnp.bfloat16), tall.astype(jnp.bfloat16), None)


def sum_nt(ones, b):
    ones = ones.astype(jnp.bfloat16)
    first, second = parts_of(b, 2)
    return nt(ones, second, None) + nt(ones, first, None)


class Unit:
    def __init__(self, index, scan, half, first, count, scanners):
        self.index, self.scan, self.half = index, scan, half
        self.first, self.count, self.share = first, count, count // scanners

    def cut(self):
        return slice(self.first, self.first + self.count)


class Exchange:
    def __init__(self, count, me, device, src, dst, sems, bulk):
        self.count, self.me, self.device = count, me, device
        self.src, self.dst, self.sems, self.bulk = src, dst, sems, bulk

    def start(self, to):
        pltpu.make_async_remote_copy(
            src_ref=self.src(to),
            dst_ref=self.dst(self.me),
            send_sem=self.sems.at[0],
            recv_sem=self.sems.at[1],
            device_id=self.device(to),
            device_id_type=MESH,
        ).start()

    def start_all(self):
        each(self.count, self.me, self.start)

    def whole(self, blocks):
        return pltpu.make_async_remote_copy(
            src_ref=self.bulk(blocks),
            dst_ref=self.bulk(blocks),
            send_sem=self.sems.at[0],
            recv_sem=self.sems.at[1],
            device_id=self.device(lax.rem(self.me + 1, self.count)),
            device_id_type=MESH,
        )

    def arrived(self, blocks=None):
        if self.count > 1:
            self.whole(blocks or self.count - 1).wait_recv()

    def sent(self, blocks=None):
        if self.count > 1:
            self.whole(blocks or self.count - 1).wait_send()


def each(count, me, act):
    if count % 2 == 0:
        act(lax.rem(me + count // 2, count))
    for j in range((count - 1) // 2, 0, -1):
        act(lax.rem(me + j, count))
        act(lax.rem(me + count - j, count))


def rows(index, size):
    return pl.ds(pl.multiple_of(index * size, size), size)


def kernel(
    nh, nx, nz, groups,
    rate_hbm, skip_hbm, x_hbm, dy_hbm, write_hbm, read_hbm, step_hbm,
    dx_ref, dwrite_ref, dread_ref, dstep_ref,
    rate_ref, skip_ref, write_ref, read_ref, step_ref,
    xg, dyg, bg, cg, pack_out, pack_in,
    cum_ref, wide_cum, grow, wide_step, wide_weight,
    decay_top, decay_low, score_top, score_low, grad_top, grad_low, row_sums,
    summed, dx_buf,
    locals_ref, scan_in, total_send, total_in, prefix, products, turned, ends,
    decay_out, decay_in, line_out, line_in,
    db_half, db_got, db_sum, db_in, dc_half, dc_got, dc_sum, dc_in,
    sems, pack_sems, own_sems,
):
    tok = step_ref.shape[0]
    heads = step_ref.shape[1]
    hl = heads // nh
    nc = nh // 2
    width = hl * WIDTH
    total = nh * tok
    low = total // 2
    pairs = hl // 2
    hh = hl // 2
    part = hh * WIDTH
    tail_rows = tok + hl
    me = lax.axis_index("head")
    at = lax.axis_index("ctx")
    my = me // 2
    core = lax.rem(me, 2)
    sibling = 1 - core
    mx = at // nz
    mz = lax.rem(at, nz)
    of_group = heads // groups

    def by_head(other):
        return {"head": other}

    def by_chip(other):
        return {"head": other * 2 + core}

    def by_core(other):
        return {"head": my * 2 + other}

    def by_z(other):
        return {"ctx": mx * nz + other}

    def by_x(other):
        return {"ctx": other * nz + mz}

    barrier = pltpu.get_barrier_semaphore()

    fetches = [
        pltpu.make_async_copy(src, dst, own_sems.at[3 + i])
        for i, (src, dst) in enumerate(
            (
                (step_hbm, step_ref),
                (write_hbm, write_ref),
                (read_hbm, read_ref),
                (rate_hbm, rate_ref),
                (skip_hbm, skip_ref),
            )
        )
    ]

    def greet(device):
        return lambda other: pl.semaphore_signal(
            barrier, inc=1, device_id=device(other), device_id_type=MESH
        )

    each(nh, me, greet(by_head))
    each(nz, mz, greet(by_z))
    if nx > 1:
        each(nx, mx, greet(by_x))
    for fetch in fetches:
        fetch.start()

    def columns(ref):
        return lambda other: ref.at[:, rows(other, width)]

    def some_columns(ref, first, size):
        return lambda other: ref.at[
            :, pl.ds(pl.multiple_of(other * width + first, size), size)
        ]

    def some_block(ref, first, size):
        return lambda other: ref.at[rows(other, tok), first : first + size]

    def block(ref, size):
        return lambda other: ref.at[rows(other, size), :]

    def along_head(src, dst, which, bulk):
        return Exchange(nh, me, by_head, src, dst, sems.at[which], bulk)

    def along_chip(src, dst, which, bulk):
        return Exchange(nc, my, by_chip, src, dst, sems.at[which], bulk)

    def across_core(src, dst, which, bulk):
        return Exchange(2, core, by_core, src, dst, sems.at[which], bulk)

    def first_rows(ref, size, cut=(0, None)):
        if cut[1] is None:
            return lambda n: ref.at[: n * size, :]
        return lambda n: ref.at[: n * size, cut[0] : cut[0] + cut[1]]

    halves = ((0, part), (part, part))
    ex_dy = [
        along_head(
            some_columns(dy_hbm, *cut), some_block(dyg, *cut), i, first_rows(dyg, tok, cut)
        )
        for i, cut in enumerate(halves)
    ]
    ex_dx = [
        along_head(
            some_block(dx_buf, *cut), some_columns(dx_ref, *cut), 2 + i,
            first_rows(dx_buf, tok, cut),
        )
        for i, cut in enumerate(halves)
    ]
    ex_x = [
        along_head(
            some_columns(x_hbm, *cut), some_block(xg, *cut), 4 + i, first_rows(xg, tok, cut)
        )
        for i, cut in enumerate(
            ((0, part), (part, part // 2), (part + part // 2, part // 2))
        )
    ]
    ex_db = along_chip(block(db_sum, tok), block(db_in, tok), 7, first_rows(db_in, tok))
    ex_dc = along_chip(
        block(dc_sum, tail_rows), block(dc_in, tail_rows), 8, first_rows(dc_in, tail_rows)
    )
    pair_pack = across_core(
        lambda t: pack_out.at[my], lambda s: pack_in.at[2 * my + s], 9, lambda n: pack_in.at[0]
    )
    pair_db = across_core(lambda t: db_half.at[t], lambda s: db_got, 10, lambda n: db_got)
    pair_dc = across_core(lambda t: dc_half.at[t], lambda s: dc_got, 11, lambda n: dc_got)
    relay = Exchange(
        nc, my, lambda t: by_core(sibling),
        lambda s: pack_in.at[2 * s + core], lambda s: None, sems.at[12],
        lambda n: pack_in.at[:n],
    )

    def pack_copy(to, slot):
        return pltpu.make_async_remote_copy(
            src_ref=pack_out.at[to],
            dst_ref=pack_in.at[2 * slot + core],
            send_sem=pack_sems.at[0],
            recv_sem=pack_sems.at[1 + slot],
            device_id=by_chip(to),
            device_id_type=MESH,
        )

    def packs_sent():
        if nc > 1:
            pltpu.make_async_remote_copy(
                src_ref=pack_out.at[: nc - 1],
                dst_ref=pack_out.at[: nc - 1],
                send_sem=pack_sems.at[0],
                recv_sem=pack_sems.at[1],
                device_id=by_chip(my),
                device_id_type=MESH,
            ).wait_send()

    grads_a = Unit(0, 1, 0, 0, part, hh)
    grads_b = Unit(1, 1, 1, part, part, hh)
    states_a = Unit(2, 0, 0, 0, part, hh)
    states_b = Unit(3, 0, 1, part, part // 2, hh)
    states_c = Unit(4, 0, 1, part + part // 2, part // 2, hh)
    my_half = lax.rem(mz, 2)

    def rows_of(u, i):
        return pl.ds(pl.multiple_of(u.first + i * u.share, u.share), u.share)

    def my_rows(u):
        return rows_of(u, mz // 2)

    def to_scanner(u):
        return Exchange(
            nz, mz, by_z,
            lambda t: locals_ref.at[u.scan, rows_of(u, t // 2), :],
            lambda s: scan_in.at[u.index, s, : u.share, :],
            sems.at[13 + u.index],
            lambda n: scan_in.at[u.index, :n, : u.share, :],
        )

    def from_scanner(u):
        return Exchange(
            nz, mz, by_z,
            lambda t: turned.at[u.index, t, : u.share, :],
            lambda s: ends.at[u.scan, my_rows(u), :],
            sems.at[18 + u.index],
            lambda n: turned.at[u.index, :n, : u.share, :],
        )

    def ex_total(u):
        return Exchange(
            nx, mx, by_x,
            lambda t: total_send.at[u.index, : u.share, :],
            lambda s: total_in.at[u.index, s, : u.share, :],
            sems.at[23 + u.index],
            lambda n: total_in.at[u.index, :n, : u.share, :],
        )

    ex_decay = Exchange(
        nz, mz, by_z, lambda t: decay_out, lambda s: decay_in.at[s], sems.at[28],
        lambda n: decay_in.at[:n],
    )
    ex_line_decay = Exchange(
        nx, mx, by_x, lambda t: line_out, lambda s: line_in.at[s], sems.at[29],
        lambda n: line_in.at[:n],
    )

    def by_half(half, act):
        @pl.when(my_half == half)
        def _():
            if hh > 1:
                act(hh - 1)

        @pl.when(my_half != half)
        def _():
            act(hh)

    def scanners(half, act):
        for j in range(hh):
            i = lax.rem(mz // 2 + hh // 2 + j, hh)

            @pl.when(2 * i + half != mz)
            def _(z=2 * i + half):
                act(z)

    own_dy = pltpu.make_async_copy(columns(dy_hbm)(me), block(dyg, tok)(me), own_sems.at[0])
    own_x = pltpu.make_async_copy(columns(x_hbm)(me), block(xg, tok)(me), own_sems.at[1])
    own_dy.start()
    own_x.start()
    for fetch in fetches:
        fetch.wait()
    padded = jnp.concatenate([step_ref[...], jnp.zeros((heads - tok, heads), F32)], axis=0)
    flipped = jnp.transpose(padded)
    for target in range(nc):
        g = target * 2 * hl // of_group
        pack_out[target, :tok, :] = write_ref[:, g * STATE : (g + 1) * STATE]
        pack_out[target, tok : 2 * tok, :] = read_ref[:, g * STATE : (g + 1) * STATE]
        first = target * 2 * hl
        pack_out[target, 2 * tok :, :heads] = flipped[first : first + hl, :] + pltpu.roll(
            flipped[first + hl : first + 2 * hl, :], tok, 1
        )
    pack_in[me] = pack_out[my]

    pl.semaphore_wait(barrier, (nh - 1) + (nz - 1) + (nx - 1))

    pair_pack.start(sibling)
    each(nc, my, lambda to: pack_copy(to, my).start())
    for exchange in ex_dy:
        exchange.start_all()

    def hand_on(chip):
        pack_copy(chip, chip).wait_recv()
        pltpu.make_async_remote_copy(
            src_ref=pack_in.at[2 * chip + core],
            dst_ref=pack_in.at[2 * chip + core],
            send_sem=sems.at[12, 0],
            recv_sem=sems.at[12, 1],
            device_id=by_core(sibling),
            device_id_type=MESH,
        ).start()

    each(nc, my, hand_on)
    for exchange in ex_x:
        exchange.start_all()
    pair_pack.arrived()
    relay.arrived()
    bg[...] = pack_in[:, :tok, :].reshape(total, STATE)
    cg[...] = pack_in[:, tok : 2 * tok, :].reshape(total, STATE)

    per_tile = heads // tok
    lane_h = lax.broadcasted_iota(jnp.int32, (hl, heads), 1) // tok
    tiles = []
    for first_source in range(0, nh, per_tile):
        tile = jnp.zeros((hl, heads), F32)
        for source in range(first_source, min(nh, first_source + per_tile)):
            spot = source - first_source
            piece = pack_in[source, 2 * tok :, :heads]
            both = []
            for c in range(2):
                shift = (heads + tok * (spot - c)) % heads
                both.append(pltpu.roll(piece, shift, 1) if shift else piece)
            tile = jnp.where(lane_h == spot, jnp.where(core == 0, both[0], both[1]), tile)
        tiles.append(tile)
    step = jnp.concatenate(tiles, axis=1)[:, :total]
    place = lax.broadcasted_iota(jnp.int32, (hl, 1), 0)
    rate = jnp.zeros((hl, 1), F32)
    for h in range(hl):
        rate = jnp.where(place == h, rate_ref[h], rate)
    lane = lax.broadcasted_iota(jnp.int32, (1, width), 1)
    skip = jnp.zeros((1, width), F32)
    for h in range(hl):
        skip = jnp.where(lane // WIDTH == h, skip_ref[h], skip)
    row_at = lax.broadcasted_iota(jnp.int32, (total, total), 0)
    col_at = lax.broadcasted_iota(jnp.int32, (total, total), 1)
    cumul = exact_nn(-step * rate, (col_at >= row_at).astype(F32))
    cum_ref[...] = cumul
    tail = jnp.exp(cumul[:, total - 1 : total])
    spread = (
        lax.broadcasted_iota(jnp.int32, (hl, width), 1) // WIDTH
        == lax.broadcasted_iota(jnp.int32, (hl, width), 0)
    ).astype(F32)
    wide = exact_tn(cumul, spread)
    wide_cum[...] = wide
    grow[...] = jnp.exp(wide)
    wide_weight[...] = jnp.exp(wide[total - 1 : total, :] - wide)
    wide_step[...] = exact_tn(step, spread)
    decay_out[...] = jnp.broadcast_to(tail, (hl, STATE))
    ex_decay.start_all()
    decay_in[mz] = decay_out[...]
    left_lanes = lax.broadcasted_iota(jnp.int32, (total, 2 * WIDTH), 1) < WIDTH
    later = lax.broadcasted_iota(jnp.int32, (low, low), 1) >= lax.broadcasted_iota(
        jnp.int32, (low, low), 0
    )

    def pair_cols(pair):
        return rows(pair, 2 * WIDTH)

    def masked(gap):
        return jnp.where(later, jnp.exp(jnp.where(later, gap, 0.0)), 0.0)

    def fill_decays(pair, carry):
        here = wide_cum[:, pair_cols(pair)]
        turned_round = pltpu.roll(here, WIDTH, 1)
        for side in range(2):
            h = 2 * pair + side
            col = jnp.where(left_lanes == (side == 0), here, turned_round)[:, :low]
            row = cum_ref[pl.ds(h, 1), :]
            decay_top[h, :, :low] = masked(row[:, :low] - col[:low, :])
            decay_top[h, :, low:] = jnp.exp(row[:, low:] - col[:low, :])
            decay_low[h] = masked(row[:, low:] - col[low:, :])
        return carry

    def send_local(u, local):
        locals_ref[u.scan, u.cut(), :] = local
        scanners(u.half, to_scanner(u).start)

        @pl.when(my_half == u.half)
        def _():
            scan_in[u.index, mz, : u.share, :] = locals_ref[u.scan, my_rows(u), :]

    def line_decays():
        ex_decay.arrived()
        product = decay_in[0]
        for z in range(1, nz):
            product = product * decay_in[z]
        line_out[...] = product
        line_in[mx] = product
        if nx > 1:
            ex_line_decay.start_all()
            ex_line_decay.arrived()

    def scan_line(u):
        @pl.when(my_half == u.half)
        def _():
            head = pl.ds((u.first + mz // 2 * u.share) // WIDTH, 1)
            to_scanner(u).arrived()
            state = jnp.zeros((u.share, STATE), F32)
            product = jnp.ones((1, STATE), F32)
            for lap in range(nz):
                z = nz - 1 - lap if u.scan else lap
                prefix[u.index, z, : u.share, :] = state
                products[u.index, z] = jnp.broadcast_to(product, (8, STATE))
                factor = decay_in[z, head, :]
                state = factor * state + scan_in[u.index, z, : u.share, :]
                product = product * factor
            total_send[u.index, : u.share, :] = state
            if nx > 1:
                ex_total(u).start_all()

    def scan_turn(u):
        @pl.when(my_half == u.half)
        def _():
            head = pl.ds((u.first + mz // 2 * u.share) // WIDTH, 1)
            state = jnp.zeros((u.share, STATE), F32)
            if nx > 1:
                total_in[u.index, mx, : u.share, :] = total_send[u.index, : u.share, :]
                ex_total(u).arrived()
                for lap in range(nx):
                    x = nx - 1 - lap if u.scan else lap
                    before = x > mx if u.scan else x < mx
                    moved = line_in[x, head, :] * state + total_in[u.index, x, : u.share, :]
                    state = jnp.where(before, moved, state)

            def turn(z):
                turned[u.index, z, : u.share, :] = (
                    prefix[u.index, z, : u.share, :] + products[u.index, z, :1, :] * state
                )

            def turn_to(z):
                turn(z)
                from_scanner(u).start(z)

            each(nz, mz, turn_to)
            turn(mz)
            ends[u.scan, my_rows(u), :] = turned[u.index, mz, : u.share, :]

    def scan_arrived(u):
        by_half(u.half, from_scanner(u).arrived)

    def scan_sent(u):
        by_half(u.half, to_scanner(u).sent)

        @pl.when(my_half == u.half)
        def _():
            ex_total(u).sent()
            from_scanner(u).sent()

    def send_grad(u):
        cols = u.cut()
        ex_dy[u.half].arrived()
        send_local(u, tn(grow[:, cols] * dyg[:, cols], cg[...]))

    def send_state(u):
        cols = u.cut()
        ex_x[u.index - 2].arrived()
        send_local(u, tn(wide_weight[:, cols] * wide_step[:, cols] * xg[:, cols], bg[...]))

    def send_dx(u):
        scan_arrived(u)
        cols = u.cut()
        whole = summed[:, cols] + wide_weight[:, cols] * nt(bg[...], ends[1, cols, :])
        summed[:, cols] = whole
        dx_buf[:, cols] = wide_step[:, cols] * whole + skip[:, cols] * dyg[:, cols]
        ex_dx[u.half].start_all()

    own_dy.wait()
    send_grad(grads_a)
    score_top[...] = nt(bg[:low, :], cg[...])
    score_low[...] = nt(bg[low:, :], cg[low:, :])
    lax.fori_loop(0, pairs, fill_decays, 0)

    def fill_summed(pair, carry):
        cols = pair_cols(pair)
        grads = dyg[:, cols]
        above, below = [], []
        for side in range(2):
            h = 2 * pair + side
            above.append(nn(score_top[...] * decay_top[h], grads))
            below.append(nn(score_low[...] * decay_low[h], grads[low:, :]))
        summed[:low, cols] = jnp.where(left_lanes[:low, :], above[0], above[1])
        summed[low:, cols] = jnp.where(left_lanes[:low, :], below[0], below[1])
        return carry

    def fill_grad_score(pair, carry):
        cols = pair_cols(pair)
        grads = dyg[:, cols]
        scaled = wide_step[:, cols] * xg[:, cols]
        for side in range(2):
            h = 2 * pair + side
            one = jnp.where(left_lanes == (side == 0), scaled, 0.0)
            above = nt(one[:low, :], grads) * decay_top[h]
            below = nt(one[low:, :], grads[low:, :]) * decay_low[h]
            grad_top[...] += above
            grad_low[...] += below
            sums = jnp.sum(above * score_top[...], axis=0, keepdims=True)
            more = jnp.sum(below * score_low[...], axis=0, keepdims=True)
            mine = lax.broadcasted_iota(jnp.int32, (hl, low), 0) == h
            row_sums[:, :low] += jnp.where(mine, sums[:, :low], 0.0)
            row_sums[:, low:] += jnp.where(mine, sums[:, low:] + more, 0.0)
        return carry

    grad_top[...] = jnp.zeros_like(grad_top)
    grad_low[...] = jnp.zeros_like(grad_low)
    row_sums[...] = jnp.zeros_like(row_sums)
    line_decays()
    send_grad(grads_b)
    lax.fori_loop(0, pairs // 2, fill_summed, 0)
    scan_line(grads_a)
    own_x.wait()
    send_state(states_a)
    scan_turn(grads_a)
    scan_line(grads_b)
    send_state(states_b)
    send_state(states_c)
    lax.fori_loop(pairs // 2, pairs, fill_summed, 0)
    scan_turn(grads_b)
    scan_line(states_a)
    send_dx(grads_a)
    scan_turn(states_a)
    scan_line(states_b)
    scan_line(states_c)
    lax.fori_loop(0, pairs // 2, fill_grad_score, 0)
    scan_turn(states_b)
    scan_turn(states_c)
    send_dx(grads_b)
    lax.fori_loop(pairs // 2, pairs, fill_grad_score, 0)
    end = ends[1]
    along = sum_nt(spread, xg[...] * summed[...])

    def by_target_core(half, stride, first, value):
        size = value.shape[0] // nh
        for target in range(nh):
            base = (target // 2) * stride + first
            half[target % 2, base : base + size, :] = value[target * size : (target + 1) * size, :]

    from_states = nn(wide_weight[...] * wide_step[...] * xg[...], end)
    by_target_core(db_half, tok, 0, from_states + jnp.concatenate(
        [nn(grad_top[...], cg[...]), nn(grad_low[...], cg[low:, :])], axis=0
    ))
    pair_db.start(sibling)
    from_score = jnp.concatenate(
        [
            tn(grad_top[:, :low], bg[:low, :]),
            tn(grad_top[:, low:], bg[:low, :]) + tn(grad_low[...], bg[low:, :]),
        ],
        axis=0,
    )
    outer = grow[...] * dyg[...]
    made = jnp.sum((end * locals_ref[0]).reshape(hl, WIDTH, STATE), axis=1)
    read_part = from_score
    along_read = row_sums[...] - step * along
    for u in (states_a, states_b, states_c):
        scan_arrived(u)
        start = ends[0, u.cut(), :]
        read_part = read_part + nn(outer[:, u.cut()], start)
        along_read = along_read + sum_nt(
            spread[:, u.cut()], outer[:, u.cut()] * nt(cg[...], start)
        )
    by_target_core(dc_half, tail_rows, 0, read_part)
    kept = jnp.sum((end * ends[0]).reshape(hl, WIDTH, STATE), axis=1)
    last = jnp.sum(tail * kept + made, axis=1, keepdims=True)
    lane_t = lax.broadcasted_iota(jnp.int32, (hl, total), 1)
    grad_cum = along_read + jnp.where(lane_t == total - 1, last, 0.0)
    grad_log = exact_nn(grad_cum, (row_at >= col_at).astype(F32))
    grad_step = along - rate * grad_log
    for target in range(nh):
        tile = target // per_tile
        begin = tile * heads
        piece = grad_step[:, begin : min(total, begin + heads)]
        if piece.shape[1] < heads:
            piece = jnp.concatenate(
                [piece, jnp.zeros((hl, heads - piece.shape[1]), F32)], axis=1
            )
        placed = []
        for c in range(2):
            shift = (heads + tok * c - tok * (target - tile * per_tile)) % heads
            placed.append(pltpu.roll(piece, shift, 1) if shift else piece)
        base = (target // 2) * tail_rows + tok
        dc_half[target % 2, base : base + hl, :heads] = jnp.where(
            lane_h == core, jnp.where(core == 0, placed[0], placed[1]), 0.0
        )
    pair_dc.start(sibling)
    pair_db.arrived()
    db_sum[...] = db_half[core] + db_got[...]
    ex_db.start_all()
    db_in[rows(my, tok), :] = db_sum[rows(my, tok), :]
    pair_dc.arrived()
    dc_sum[...] = dc_half[core] + dc_got[...]
    ex_dc.start_all()
    dc_in[rows(my, tail_rows), :] = dc_sum[rows(my, tail_rows), :]

    share = nc // groups

    def fold(received, stride, out):
        for g in range(groups):
            part = received[g * share * stride : g * share * stride + tok, :]
            for s in range(g * share + 1, (g + 1) * share):
                part = part + received[s * stride : s * stride + tok, :]
            out[:, g * STATE : (g + 1) * STATE] = part

    dx_ref[:, rows(me, width)] = dx_buf[rows(me, tok), :]
    for exchange in (*ex_dy, *ex_x, *ex_dx, relay, ex_decay, ex_line_decay):
        exchange.sent()
    packs_sent()
    for u in (grads_a, grads_b, states_a, states_b, states_c):
        scan_sent(u)
    for exchange in (pair_pack, pair_db, pair_dc):
        exchange.sent()
    for exchange in ex_dx:
        exchange.arrived()
    ex_db.arrived()
    fold(db_in, tok, dwrite_ref)
    ex_db.sent()
    ex_dc.arrived()
    fold(dc_in, tail_rows, dread_ref)
    by_heads = []
    for chip in range(nc):
        piece = dc_in[chip * tail_rows + tok : (chip + 1) * tail_rows, :heads]
        by_heads += [piece, pltpu.roll(piece, heads - tok, 1)]
    dstep_ref[...] = jnp.transpose(jnp.concatenate(by_heads, axis=0))[:tok, :]
    ex_dc.sent()


def hand_out(count, *refs):
    for i in range(count):
        refs[count + i][...] = refs[i][...]


def on_device(groups, features, write_proj, read_proj, step_size, decay_rate, skip_weight, upstream):
    nh = lax.axis_size("head")
    tok, heads = step_size.shape
    hl = heads // nh
    nz = hl
    nx = lax.axis_size("ctx") // nz
    width = hl * WIDTH
    nc = nh // 2
    total = nh * tok
    low = total // 2
    vmem = pl.BlockSpec(memory_space=pltpu.VMEM)
    hbm = pl.BlockSpec(memory_space=pltpu.HBM)

    def buf(*shape):
        return pltpu.VMEM(shape, F32)

    results = pl.pallas_call(
        functools.partial(kernel, nh, nx, nz, groups),
        out_shape=(
            jax.ShapeDtypeStruct(features.shape, F32),
            jax.ShapeDtypeStruct(write_proj.shape, F32),
            jax.ShapeDtypeStruct(read_proj.shape, F32),
            jax.ShapeDtypeStruct(step_size.shape, F32),
        ),
        in_specs=[hbm] * 7,
        out_specs=(vmem, vmem, vmem, vmem),
        scratch_shapes=[
            pltpu.SMEM(decay_rate.shape, F32),
            pltpu.SMEM(skip_weight.shape, F32),
            buf(*write_proj.shape),
            buf(*read_proj.shape),
            buf(*step_size.shape),
            buf(total, width),
            buf(total, width),
            buf(total, STATE),
            buf(total, STATE),
            buf(nc, 2 * tok + hl, STATE),
            buf(nh, 2 * tok + hl, STATE),
            buf(hl, total),
            buf(total, width),
            buf(total, width),
            buf(total, width),
            buf(total, width),
            buf(hl, low, total),
            buf(hl, low, low),
            buf(low, total),
            buf(low, low),
            buf(low, total),
            buf(low, low),
            buf(hl, total),
            buf(total, width),
            buf(total, width),
            buf(2, hl * WIDTH, STATE),
            buf(5, nz, WIDTH, STATE),
            buf(5, WIDTH, STATE),
            buf(5, nx, WIDTH, STATE),
            buf(5, nz, WIDTH, STATE),
            buf(5, nz, 8, STATE),
            buf(5, nz, WIDTH, STATE),
            buf(2, hl * WIDTH, STATE),
            buf(hl, STATE),
            buf(nz, hl, STATE),
            buf(hl, STATE),
            buf(nx, hl, STATE),
            buf(2, nc * tok, STATE),
            buf(nc * tok, STATE),
            buf(nc * tok, STATE),
            buf(nc * tok, STATE),
            buf(2, nc * (tok + hl), STATE),
            buf(nc * (tok + hl), STATE),
            buf(nc * (tok + hl), STATE),
            buf(nc * (tok + hl), STATE),
            pltpu.SemaphoreType.DMA((30, 2)),
            pltpu.SemaphoreType.DMA((1 + nc,)),
            pltpu.SemaphoreType.DMA((8,)),
        ],
        compiler_params=pltpu.CompilerParams(
            collective_id=0, has_side_effects=True, vmem_limit_bytes=64 * 1024 * 1024
        ),
        cost_estimate=pl.CostEstimate(
            flops=1_200_000_000, bytes_accessed=8_000_000, transcendentals=600_000
        ),
    )(decay_rate, skip_weight, features, upstream, write_proj, read_proj, step_size)
    return pl.pallas_call(
        functools.partial(hand_out, len(results)),
        out_shape=tuple(jax.ShapeDtypeStruct(r.shape, F32) for r in results),
        in_specs=[vmem] * len(results),
        out_specs=(vmem,) * len(results),
        compiler_params=pltpu.CompilerParams(vmem_limit_bytes=64 * 1024 * 1024),
        cost_estimate=pl.CostEstimate(flops=0, bytes_accessed=1_200_000, transcendentals=0),
    )(*results)


def solution(mesh):
    tokens = P(("ctx", "head"), None)
    return jax.shard_map(
        functools.partial(on_device, GROUPS),
        mesh=mesh,
        in_specs=(tokens, tokens, tokens, tokens, P("head"), P("head"), tokens),
        out_specs=(tokens, tokens, tokens, tokens),
        check_vma=False,
    )
```

time: 420 us -> 73.3 us (0.17)
  waiting for transfers between devices: 174 us -> 0 us
  blocking collectives: 84.7 us -> 0 us
  Pallas kernels: 0 us -> 72.5 us
  local copies, waits for them, and re-layouts: 70.8 us -> 0 us
  starting transfers between devices: 37 us -> 0 us
  matrix products: 22.1 us -> 0 us
  between operations: 14.6 us -> 0.64 us
  other arithmetic: 12.4 us -> 0 us
    all_gather x2 -> x0, waiting for transfers between devices: 127 us -> none  [entering_2(): gathered = jax.tree.map(lambda a: lax.all_gather(a, axis), part)]
    all_gather x3 -> x0, blocking collectives: 84.7 us -> none  [the longest x1 39.2 us: entering_2(): gathered = jax.tree.map(lambda a: lax.all_gather(a, axis), part)]
    pallas_call x0 -> x2, Pallas kernels: none -> 72.5 us  [the longest x1 70.6 us: on_device(): pl.pallas_call(functools.partial(kernel, nh, nx, nz, groups), out_shape=(...]
    all_to_all x7 -> x0, waiting for transfers between devices: 47.2 us -> none  [the longest x1 14.5 us: on_device(): lax.all_to_all(grad_feat.reshape(rows_all, head_local * width), 'head', s...]
    all_to_all x7 -> x0, starting transfers between devices: 37 us -> none  [the longest x1 10.1 us: on_device(): lax.all_to_all(step_size, 'head', split_axis=1, concat_axis=0, tiled=True)]
    dynamic_slice x64 -> x0, local copies, waits for them, and re-layouts: 36.6 us -> none  [the longest x62 36.4 us: one(): lax.dynamic_index_in_dim(a, source, 0, False)]
    dot_general x13 -> x0, matrix products: 22.1 us -> none  [the longest x1 3.71 us: on_device(): jnp.einsum('bihp,bjhp->bhij', grad_y, scaled, precision=high) * lower_f]
    mul x33 -> x0, local copies, waits for them, and re-layouts: 21.4 us -> none  [the longest x31 21.3 us: backward_combine(): later[0][:, None, None] * earlier[1]]
  transfers between devices with their start and end apart: 9 -> 0, of which waited for: 7 -> 0; matrix products, arithmetic and copies ran while one was open for 6% -> 0% of each run, Pallas kernels for 0% -> 0%
where the time goes in v1:
time: 73.3 us; the launch traced here: 73.1 us
  Pallas kernels  72.5 us (99%)
    pallas_call x1, Pallas kernels, on_device(): pl.pallas_call(functools.partial(kernel, nh, nx, nz, groups), out_shape=(...  70.6 us
    pallas_call x1, Pallas kernels, on_device(): pl.pallas_call(functools.partial(hand_out, len(results)), out_shape=tuple...  1.9 us

profile of v1, /device:TPU:1, one launch (start us, length us, event | category | flops | bytes accessed | tf_op | source)
XLA Modules:
  0.0 73.1 jit_solution(362568924362009865)
XLA Ops:
  0.6 70.6 %shard_map.102 = (f32[16,8192]{1,0:T(8,128)}, f32[16,512]{1,0:T(8,128)}, f32[16,512]{1,0:T(8,128)}, f32[16,128]{1,0:T(8,128)}) custom-call(f32[8]{0:T(128)} %rate_hbm.1, f32[8]{0:T(128)} %skip_hbm.1, f32[16,8192]{1,0:T(8,128)} %x_hbm.1, f32[16,8192]{1,0:T(8,128)} %dy_hbm.1, f32[16,512]{1,0:T(8,128)} %write_hbm.1, f32[16,512]{1,0:T(8,128)} %read_hbm.1, ...), custom_call_target="tpu_custom_call" | custom-call | flops 1200000000 | bytes 8000000 | tf_op jit(solution)/shard_map/pallas_call | solution.py:730
  71.2 1.9 %shard_map.103 = (f32[16,8192]{1,0:T(8,128)}, f32[16,512]{1,0:T(8,128)}, f32[16,512]{1,0:T(8,128)}, f32[16,128]{1,0:T(8,128)}) custom-call(f32[16,8192]{1,0:T(8,128)} %get-tuple-element.8.refs_0_, f32[16,512]{1,0:T(8,128)} %get-tuple-element.9.refs_1_, f32[16,512]{1,0:T(8,128)} %get-tuple-element.10.refs_2_, f32[16,128]{1,0:T(8,128)} %get-tuple-element.11.refs_3_), custom_call_target="tpu_custom_call" | custom-call | bytes 1200000 | tf_op jit(solution)/shard_map/pallas_call | solution.py:797

commit v2 on v1

--- a/solution.py
+++ b/solution.py
@@ -122,12 +122,12 @@
 def kernel(
     nh, nx, nz, groups,
     rate_hbm, skip_hbm, x_hbm, dy_hbm, write_hbm, read_hbm, step_hbm,
-    dx_ref, dwrite_ref, dread_ref, dstep_ref,
+    dx_hbm, dwrite_ref, dread_ref, dstep_ref,
     rate_ref, skip_ref, write_ref, read_ref, step_ref,
     xg, dyg, bg, cg, pack_out, pack_in,
     cum_ref, wide_cum, grow, wide_step, wide_weight,
     decay_top, decay_low, score_top, score_low, grad_top, grad_low, row_sums,
-    summed, dx_buf,
+    summed, dx_buf, dx_ref,
     locals_ref, scan_in, total_send, total_in, prefix, products, turned, ends,
     decay_out, decay_in, line_out, line_in,
     db_half, db_got, db_sum, db_in, dc_half, dc_got, dc_sum, dc_in,
@@ -557,31 +557,37 @@
     def fill_summed(pair, carry):
         cols = pair_cols(pair)
         grads = dyg[:, cols]
-        above, below = [], []
-        for side in range(2):
-            h = 2 * pair + side
-            above.append(nn(score_top[...] * decay_top[h], grads))
-            below.append(nn(score_low[...] * decay_low[h], grads[low:, :]))
-        summed[:low, cols] = jnp.where(left_lanes[:low, :], above[0], above[1])
-        summed[low:, cols] = jnp.where(left_lanes[:low, :], below[0], below[1])
+        heads_of = (2 * pair, 2 * pair + 1)
+        above = nn(
+            jnp.concatenate([score_top[...] * decay_top[h] for h in heads_of], axis=0), grads
+        )
+        below = nn(
+            jnp.concatenate([score_low[...] * decay_low[h] for h in heads_of], axis=0),
+            grads[low:, :],
+        )
+        summed[:low, cols] = jnp.where(left_lanes[:low, :], above[:low, :], above[low:, :])
+        summed[low:, cols] = jnp.where(left_lanes[:low, :], below[:low, :], below[low:, :])
         return carry
 
     def fill_grad_score(pair, carry):
         cols = pair_cols(pair)
         grads = dyg[:, cols]
         scaled = wide_step[:, cols] * xg[:, cols]
+        sides = [jnp.where(left_lanes == (side == 0), scaled, 0.0) for side in range(2)]
+        above = nt(jnp.concatenate([one[:low, :] for one in sides], axis=0), grads)
+        below = nt(jnp.concatenate([one[low:, :] for one in sides], axis=0), grads[low:, :])
+        mixed_top, mixed_low = [], []
         for side in range(2):
             h = 2 * pair + side
-            one = jnp.where(left_lanes == (side == 0), scaled, 0.0)
-            above = nt(one[:low, :], grads) * decay_top[h]
-            below = nt(one[low:, :], grads[low:, :]) * decay_low[h]
-            grad_top[...] += above
-            grad_low[...] += below
-            sums = jnp.sum(above * score_top[...], axis=0, keepdims=True)
-            more = jnp.sum(below * score_low[...], axis=0, keepdims=True)
+            mixed_top.append(above[side * low : (side + 1) * low, :] * decay_top[h])
+            mixed_low.append(below[side * low : (side + 1) * low, :] * decay_low[h])
+            sums = jnp.sum(mixed_top[side] * score_top[...], axis=0, keepdims=True)
+            more = jnp.sum(mixed_low[side] * score_low[...], axis=0, keepdims=True)
             mine = lax.broadcasted_iota(jnp.int32, (hl, low), 0) == h
             row_sums[:, :low] += jnp.where(mine, sums[:, :low], 0.0)
             row_sums[:, low:] += jnp.where(mine, sums[:, low:] + more, 0.0)
+        grad_top[...] += mixed_top[0] + mixed_top[1]
+        grad_low[...] += mixed_low[0] + mixed_low[1]
         return carry
 
     grad_top[...] = jnp.zeros_like(grad_top)
@@ -604,11 +610,11 @@
     scan_turn(states_a)
     scan_line(states_b)
     scan_line(states_c)
-    lax.fori_loop(0, pairs // 2, fill_grad_score, 0)
+    lax.fori_loop(0, pairs - 1, fill_grad_score, 0)
     scan_turn(states_b)
     scan_turn(states_c)
     send_dx(grads_b)
-    lax.fori_loop(pairs // 2, pairs, fill_grad_score, 0)
+    lax.fori_loop(pairs - 1, pairs, fill_grad_score, 0)
     end = ends[1]
     along = sum_nt(spread, xg[...] * summed[...])
 
@@ -634,36 +640,38 @@
     made = jnp.sum((end * locals_ref[0]).reshape(hl, WIDTH, STATE), axis=1)
     read_part = from_score
     along_read = row_sums[...] - step * along
+    kept = []
     for u in (states_a, states_b, states_c):
         scan_arrived(u)
         start = ends[0, u.cut(), :]
+        kept.append(
+            jnp.sum((end[u.cut(), :] * start).reshape(u.count // WIDTH, WIDTH, STATE), axis=1)
+        )
         read_part = read_part + nn(outer[:, u.cut()], start)
         along_read = along_read + sum_nt(
             spread[:, u.cut()], outer[:, u.cut()] * nt(cg[...], start)
         )
     by_target_core(dc_half, tail_rows, 0, read_part)
-    kept = jnp.sum((end * ends[0]).reshape(hl, WIDTH, STATE), axis=1)
+    kept = jnp.concatenate(kept, axis=0)
     last = jnp.sum(tail * kept + made, axis=1, keepdims=True)
     lane_t = lax.broadcasted_iota(jnp.int32, (hl, total), 1)
     grad_cum = along_read + jnp.where(lane_t == total - 1, last, 0.0)
     grad_log = exact_nn(grad_cum, (row_at >= col_at).astype(F32))
     grad_step = along - rate * grad_log
-    for target in range(nh):
-        tile = target // per_tile
-        begin = tile * heads
+    for begin in range(0, total, heads):
         piece = grad_step[:, begin : min(total, begin + heads)]
         if piece.shape[1] < heads:
             piece = jnp.concatenate(
                 [piece, jnp.zeros((hl, heads - piece.shape[1]), F32)], axis=1
             )
-        placed = []
-        for c in range(2):
-            shift = (heads + tok * c - tok * (target - tile * per_tile)) % heads
-            placed.append(pltpu.roll(piece, shift, 1) if shift else piece)
-        base = (target // 2) * tail_rows + tok
-        dc_half[target % 2, base : base + hl, :heads] = jnp.where(
-            lane_h == core, jnp.where(core == 0, placed[0], placed[1]), 0.0
-        )
+        turns = [pltpu.roll(piece, tok * t, 1) if t else piece for t in range(per_tile)]
+        for spot in range(min(per_tile, nh)):
+            target = begin // tok + spot
+            placed = [turns[(c - spot) % per_tile] for c in range(2)]
+            base = (target // 2) * tail_rows + tok
+            dc_half[target % 2, base : base + hl, :heads] = jnp.where(
+                lane_h == core, jnp.where(core == 0, placed[0], placed[1]), 0.0
+            )
     pair_dc.start(sibling)
     pair_db.arrived()
     db_sum[...] = db_half[core] + db_got[...]
@@ -693,6 +701,8 @@
         exchange.sent()
     for exchange in ex_dx:
         exchange.arrived()
+    put_dx = pltpu.make_async_copy(dx_ref, dx_hbm, own_sems.at[2])
+    put_dx.start()
     ex_db.arrived()
     fold(db_in, tok, dwrite_ref)
     ex_db.sent()
@@ -704,11 +714,32 @@
         by_heads += [piece, pltpu.roll(piece, heads - tok, 1)]
     dstep_ref[...] = jnp.transpose(jnp.concatenate(by_heads, axis=0))[:tok, :]
     ex_dc.sent()
-
-
-def hand_out(count, *refs):
+    put_dx.wait()
+
+
+def hand_out(parts, *refs):
+    count = len(parts)
+    sems = refs[-1]
+    copies = []
     for i in range(count):
-        refs[count + i][...] = refs[i][...]
+        wide = refs[i].shape[1] // parts[i]
+        for p in range(parts[i]):
+            cols = slice(p * wide, (p + 1) * wide)
+            through = refs[2 * count + i].at[:, cols]
+            at = len(copies)
+            copies.append(
+                (
+                    pltpu.make_async_copy(refs[i].at[:, cols], through, sems.at[0, at]),
+                    pltpu.make_async_copy(through, refs[count + i].at[:, cols], sems.at[1, at]),
+                )
+            )
+    for fetch, _ in copies:
+        fetch.start()
+    for fetch, put in copies:
+        fetch.wait()
+        put.start()
+    for _, put in copies:
+        put.wait()
 
 
 def on_device(groups, features, write_proj, read_proj, step_size, decay_rate, skip_weight, upstream):
@@ -736,7 +767,7 @@
             jax.ShapeDtypeStruct(step_size.shape, F32),
         ),
         in_specs=[hbm] * 7,
-        out_specs=(vmem, vmem, vmem, vmem),
+        out_specs=(hbm, vmem, vmem, vmem),
         scratch_shapes=[
             pltpu.SMEM(decay_rate.shape, F32),
             pltpu.SMEM(skip_weight.shape, F32),
@@ -763,6 +794,7 @@
             buf(hl, total),
             buf(total, width),
             buf(total, width),
+            buf(*features.shape),
             buf(2, hl * WIDTH, STATE),
             buf(5, nz, WIDTH, STATE),
             buf(5, WIDTH, STATE),
@@ -794,11 +826,16 @@
             flops=1_200_000_000, bytes_accessed=8_000_000, transcendentals=600_000
         ),
     )(decay_rate, skip_weight, features, upstream, write_proj, read_proj, step_size)
+    parts = (4, 1, 1, 1)
     return pl.pallas_call(
-        functools.partial(hand_out, len(results)),
+        functools.partial(hand_out, parts),
         out_shape=tuple(jax.ShapeDtypeStruct(r.shape, F32) for r in results),
-        in_specs=[vmem] * len(results),
-        out_specs=(vmem,) * len(results),
+        in_specs=[hbm] * len(results),
+        out_specs=(hbm,) * len(results),
+        scratch_shapes=[
+            *(buf(*r.shape) for r in results),
+            pltpu.SemaphoreType.DMA((2, sum(parts))),
+        ],
         compiler_params=pltpu.CompilerParams(vmem_limit_bytes=64 * 1024 * 1024),
         cost_estimate=pl.CostEstimate(flops=0, bytes_accessed=1_200_000, transcendentals=0),
     )(*results)

time: 73.3 us -> 73.1 us (level)
  no operation moved by 1% of the time
where the time goes in v2:
time: 73.1 us; the launch traced here: 72.9 us
  Pallas kernels  72.3 us (99%)
    pallas_call x1, Pallas kernels, on_device(): pl.pallas_call(functools.partial(kernel, nh, nx, nz, groups), out_shape=(...  70.4 us
    pallas_call x1, Pallas kernels, on_device(): pl.pallas_call(functools.partial(hand_out, parts), out_shape=tuple((jax.S...  1.89 us

profile of v2, /device:TPU:1, one launch (start us, length us, event | category | flops | bytes accessed | tf_op | source)
XLA Modules:
  0.0 72.9 jit_solution(581257483843064994)
XLA Ops:
  0.6 70.4 %shard_map.102 = (f32[16,8192]{1,0:T(8,128)}, f32[16,512]{1,0:T(8,128)}, f32[16,512]{1,0:T(8,128)}, f32[16,128]{1,0:T(8,128)}) custom-call(f32[8]{0:T(128)} %rate_hbm.1, f32[8]{0:T(128)} %skip_hbm.1, f32[16,8192]{1,0:T(8,128)} %x_hbm.1, f32[16,8192]{1,0:T(8,128)} %dy_hbm.1, f32[16,512]{1,0:T(8,128)} %write_hbm.1, f32[16,512]{1,0:T(8,128)} %read_hbm.1, ...), custom_call_target="tpu_custom_call" | custom-call | flops 1200000000 | bytes 8000000 | tf_op jit(solution)/shard_map/pallas_call | solution.py:761
  71.0 1.9 %shard_map.103 = (f32[16,8192]{1,0:T(8,128)}, f32[16,512]{1,0:T(8,128)}, f32[16,512]{1,0:T(8,128)}, f32[16,128]{1,0:T(8,128)}) custom-call(f32[16,8192]{1,0:T(8,128)} %get-tuple-element.8.refs_0_, f32[16,512]{1,0:T(8,128)} %get-tuple-element.9.refs_1_, f32[16,512]{1,0:T(8,128)} %get-tuple-element.10.refs_2_, f32[16,128]{1,0:T(8,128)} %get-tuple-element.11.refs_3_), custom_call_target="tpu_custom_call" | custom-call | bytes 1200000 | tf_op jit(solution)/shard_map/pallas_call | solution.py:830

commit v3 on v2

--- a/solution.py
+++ b/solution.py
@@ -122,12 +122,12 @@
 def kernel(
     nh, nx, nz, groups,
     rate_hbm, skip_hbm, x_hbm, dy_hbm, write_hbm, read_hbm, step_hbm,
-    dx_hbm, dwrite_ref, dread_ref, dstep_ref,
+    dx_ref, dwrite_ref, dread_ref, dstep_ref,
     rate_ref, skip_ref, write_ref, read_ref, step_ref,
     xg, dyg, bg, cg, pack_out, pack_in,
     cum_ref, wide_cum, grow, wide_step, wide_weight,
     decay_top, decay_low, score_top, score_low, grad_top, grad_low, row_sums,
-    summed, dx_buf, dx_ref,
+    summed, dx_buf,
     locals_ref, scan_in, total_send, total_in, prefix, products, turned, ends,
     decay_out, decay_in, line_out, line_in,
     db_half, db_got, db_sum, db_in, dc_half, dc_got, dc_sum, dc_in,
@@ -691,7 +691,8 @@
                 part = part + received[s * stride : s * stride + tok, :]
             out[:, g * STATE : (g + 1) * STATE] = part
 
-    dx_ref[:, rows(me, width)] = dx_buf[rows(me, tok), :]
+    own_dx = pltpu.make_async_copy(block(dx_buf, tok)(me), columns(dx_ref)(me), own_sems.at[2])
+    own_dx.start()
     for exchange in (*ex_dy, *ex_x, *ex_dx, relay, ex_decay, ex_line_decay):
         exchange.sent()
     packs_sent()
@@ -701,8 +702,6 @@
         exchange.sent()
     for exchange in ex_dx:
         exchange.arrived()
-    put_dx = pltpu.make_async_copy(dx_ref, dx_hbm, own_sems.at[2])
-    put_dx.start()
     ex_db.arrived()
     fold(db_in, tok, dwrite_ref)
     ex_db.sent()
@@ -714,7 +713,7 @@
         by_heads += [piece, pltpu.roll(piece, heads - tok, 1)]
     dstep_ref[...] = jnp.transpose(jnp.concatenate(by_heads, axis=0))[:tok, :]
     ex_dc.sent()
-    put_dx.wait()
+    own_dx.wait()
 
 
 def hand_out(parts, *refs):
@@ -725,21 +724,15 @@
         wide = refs[i].shape[1] // parts[i]
         for p in range(parts[i]):
             cols = slice(p * wide, (p + 1) * wide)
-            through = refs[2 * count + i].at[:, cols]
-            at = len(copies)
             copies.append(
-                (
-                    pltpu.make_async_copy(refs[i].at[:, cols], through, sems.at[0, at]),
-                    pltpu.make_async_copy(through, refs[count + i].at[:, cols], sems.at[1, at]),
+                pltpu.make_async_copy(
+                    refs[i].at[:, cols], refs[count + i].at[:, cols], sems.at[len(copies)]
                 )
             )
-    for fetch, _ in copies:
-        fetch.start()
-    for fetch, put in copies:
-        fetch.wait()
-        put.start()
-    for _, put in copies:
-        put.wait()
+    for copy in copies:
+        copy.start()
+    for copy in copies:
+        copy.wait()
 
 
 def on_device(groups, features, write_proj, read_proj, step_size, decay_rate, skip_weight, upstream):
@@ -767,7 +760,7 @@
             jax.ShapeDtypeStruct(step_size.shape, F32),
         ),
         in_specs=[hbm] * 7,
-        out_specs=(hbm, vmem, vmem, vmem),
+        out_specs=(vmem, vmem, vmem, vmem),
         scratch_shapes=[
             pltpu.SMEM(decay_rate.shape, F32),
             pltpu.SMEM(skip_weight.shape, F32),
@@ -794,7 +787,6 @@
             buf(hl, total),
             buf(total, width),
             buf(total, width),
-            buf(*features.shape),
             buf(2, hl * WIDTH, STATE),
             buf(5, nz, WIDTH, STATE),
             buf(5, WIDTH, STATE),
@@ -820,25 +812,29 @@
             pltpu.SemaphoreType.DMA((8,)),
         ],
         compiler_params=pltpu.CompilerParams(
-            collective_id=0, has_side_effects=True, vmem_limit_bytes=64 * 1024 * 1024
+            collective_id=0, has_side_effects=True, vmem_limit_bytes=40 * 1024 * 1024
         ),
         cost_estimate=pl.CostEstimate(
             flops=1_200_000_000, bytes_accessed=8_000_000, transcendentals=600_000
         ),
-    )(decay_rate, skip_weight, features, upstream, write_proj, read_proj, step_size)
+    )(
+        *(
+            pltpu.with_memory_space_constraint(a, pltpu.HBM)
+            for a in (
+                decay_rate, skip_weight, features, upstream, write_proj, read_proj, step_size
+            )
+        )
+    )
     parts = (4, 1, 1, 1)
     return pl.pallas_call(
         functools.partial(hand_out, parts),
         out_shape=tuple(jax.ShapeDtypeStruct(r.shape, F32) for r in results),
-        in_specs=[hbm] * len(results),
+        in_specs=[vmem] * len(results),
         out_specs=(hbm,) * len(results),
-        scratch_shapes=[
-            *(buf(*r.shape) for r in results),
-            pltpu.SemaphoreType.DMA((2, sum(parts))),
-        ],
-        compiler_params=pltpu.CompilerParams(vmem_limit_bytes=64 * 1024 * 1024),
+        scratch_shapes=[pltpu.SemaphoreType.DMA((sum(parts),))],
+        compiler_params=pltpu.CompilerParams(vmem_limit_bytes=16 * 1024 * 1024),
         cost_estimate=pl.CostEstimate(flops=0, bytes_accessed=1_200_000, transcendentals=0),
-    )(*results)
+    )(*(pltpu.with_memory_space_constraint(r, pltpu.VMEM) for r in results))
 
 
 def solution(mesh):

time: 73.1 us -> 71.5 us (0.978)
  Pallas kernels: 72.3 us -> 70.6 us
    pallas_call x1, Pallas kernels: 1.89 us -> 0.86 us  [on_device(): pl.pallas_call(functools.partial(hand_out, parts), out_shape=tuple((jax.S...]
where the time goes in v3:
time: 71.5 us; the launch traced here: 71.3 us
  Pallas kernels  70.6 us (99%)
    pallas_call x1, Pallas kernels, on_device(): pl.pallas_call(functools.partial(kernel, nh, nx, nz, groups), out_shape=(...  69.8 us

profile of v3, /device:TPU:1, one launch (start us, length us, event | category | flops | bytes accessed | tf_op | source)
XLA Modules:
  0.0 71.3 jit_solution(6125474996987467734)
XLA Ops:
  0.6 69.8 %shard_map.102 = (f32[16,8192]{1,0:T(8,128)S(1)}, f32[16,512]{1,0:T(8,128)S(1)}, f32[16,512]{1,0:T(8,128)S(1)}, f32[16,128]{1,0:T(8,128)S(1)}) custom-call(f32[8]{0:T(128)} %rate_hbm.1, f32[8]{0:T(128)} %skip_hbm.1, f32[16,8192]{1,0:T(8,128)} %x_hbm.1, f32[16,8192]{1,0:T(8,128)} %dy_hbm.1, f32[16,512]{1,0:T(8,128)} %write_hbm.1, f32[16,512]{1,0:T(8,128)} %read_hbm.1, ...), custom_call_target="tpu_custom_call" | custom-call | flops 1200000000 | bytes 8000000 | tf_op jit(solution)/shard_map/pallas_call | solution.py:754
  70.4 0.9 %shard_map.103 = (f32[16,8192]{1,0:T(8,128)}, f32[16,512]{1,0:T(8,128)}, f32[16,512]{1,0:T(8,128)}, f32[16,128]{1,0:T(8,128)}) custom-call(f32[16,8192]{1,0:T(8,128)S(1)} %get-tuple-element.8.refs_0_, f32[16,512]{1,0:T(8,128)S(1)} %get-tuple-element.9.refs_1_, f32[16,512]{1,0:T(8,128)S(1)} %get-tuple-element.10.refs_2_, f32[16,128]{1,0:T(8,128)S(1)} %get-tuple-element.11.refs_3_), custom_call_target="tpu_custom_call" | custom-call | bytes 1200000 | tf_op jit(solution)/shard_map/pallas_call | solution.py:829

commit v4 on v3

--- a/solution.py
+++ b/solution.py
@@ -107,12 +107,16 @@
             self.whole(blocks or self.count - 1).wait_send()
 
 
+def others(count, me):
+    out = [lax.rem(me + count // 2, count)] if count % 2 == 0 else []
+    for j in range((count - 1) // 2, 0, -1):
+        out += [lax.rem(me + j, count), lax.rem(me + count - j, count)]
+    return out
+
+
 def each(count, me, act):
-    if count % 2 == 0:
-        act(lax.rem(me + count // 2, count))
-    for j in range((count - 1) // 2, 0, -1):
-        act(lax.rem(me + j, count))
-        act(lax.rem(me + count - j, count))
+    for other in others(count, me):
+        act(other)
 
 
 def rows(index, size):
@@ -188,8 +192,12 @@
             barrier, inc=1, device_id=device(other), device_id_type=MESH
         )
 
-    each(nh, me, greet(by_head))
-    each(nz, mz, greet(by_z))
+    along_y = [(by_head, other) for other in others(nh, me)]
+    along_z = [(by_z, other) for other in others(nz, mz)]
+    while along_y or along_z:
+        for device, other in along_y[:2] + along_z[:1]:
+            greet(device)(other)
+        along_y, along_z = along_y[2:], along_z[1:]
     if nx > 1:
         each(nx, mx, greet(by_x))
     for fetch in fetches:
@@ -606,17 +614,16 @@
     lax.fori_loop(pairs // 2, pairs, fill_summed, 0)
     scan_turn(grads_b)
     scan_line(states_a)
-    send_dx(grads_a)
-    scan_turn(states_a)
     scan_line(states_b)
     scan_line(states_c)
-    lax.fori_loop(0, pairs - 1, fill_grad_score, 0)
+    scan_turn(states_a)
+    send_dx(grads_a)
+    lax.fori_loop(0, pairs // 2, fill_grad_score, 0)
     scan_turn(states_b)
     scan_turn(states_c)
     send_dx(grads_b)
-    lax.fori_loop(pairs - 1, pairs, fill_grad_score, 0)
+    lax.fori_loop(pairs // 2, pairs, fill_grad_score, 0)
     end = ends[1]
-    along = sum_nt(spread, xg[...] * summed[...])
 
     def by_target_core(half, stride, first, value):
         size = value.shape[0] // nh
@@ -629,6 +636,7 @@
         [nn(grad_top[...], cg[...]), nn(grad_low[...], cg[low:, :])], axis=0
     ))
     pair_db.start(sibling)
+    along = sum_nt(spread, xg[...] * summed[...])
     from_score = jnp.concatenate(
         [
             tn(grad_top[:, :low], bg[:low, :]),
@@ -642,6 +650,11 @@
     along_read = row_sums[...] - step * along
     kept = []
     for u in (states_a, states_b, states_c):
+        if u is states_b:
+            pair_db.arrived()
+            db_sum[...] = db_half[core] + db_got[...]
+            ex_db.start_all()
+            db_in[rows(my, tok), :] = db_sum[rows(my, tok), :]
         scan_arrived(u)
         start = ends[0, u.cut(), :]
         kept.append(
@@ -673,10 +686,6 @@
                 lane_h == core, jnp.where(core == 0, placed[0], placed[1]), 0.0
             )
     pair_dc.start(sibling)
-    pair_db.arrived()
-    db_sum[...] = db_half[core] + db_got[...]
-    ex_db.start_all()
-    db_in[rows(my, tok), :] = db_sum[rows(my, tok), :]
     pair_dc.arrived()
     dc_sum[...] = dc_half[core] + dc_got[...]
     ex_dc.start_all()

time: 71.5 us -> 71.5 us (level)
  no operation moved by 1% of the time
where the time goes in v4:
time: 71.5 us; the launch traced here: 71.3 us
  Pallas kernels  70.7 us (99%)
    pallas_call x1, Pallas kernels, on_device(): pl.pallas_call(functools.partial(kernel, nh, nx, nz, groups), out_shape=(...  69.8 us

profile of v4, /device:TPU:1, one launch (start us, length us, event | category | flops | bytes accessed | tf_op | source)
XLA Modules:
  0.0 71.3 jit_solution(749587786879738710)
XLA Ops:
  0.6 69.8 %shard_map.102 = (f32[16,8192]{1,0:T(8,128)S(1)}, f32[16,512]{1,0:T(8,128)S(1)}, f32[16,512]{1,0:T(8,128)S(1)}, f32[16,128]{1,0:T(8,128)S(1)}) custom-call(f32[8]{0:T(128)} %rate_hbm.1, f32[8]{0:T(128)} %skip_hbm.1, f32[16,8192]{1,0:T(8,128)} %x_hbm.1, f32[16,8192]{1,0:T(8,128)} %dy_hbm.1, f32[16,512]{1,0:T(8,128)} %write_hbm.1, f32[16,512]{1,0:T(8,128)} %read_hbm.1, ...), custom_call_target="tpu_custom_call" | custom-call | flops 1200000000 | bytes 8000000 | tf_op jit(solution)/shard_map/pallas_call | solution.py:763
  70.5 0.9 %shard_map.103 = (f32[16,8192]{1,0:T(8,128)}, f32[16,512]{1,0:T(8,128)}, f32[16,512]{1,0:T(8,128)}, f32[16,128]{1,0:T(8,128)}) custom-call(f32[16,8192]{1,0:T(8,128)S(1)} %get-tuple-element.8.refs_0_, f32[16,512]{1,0:T(8,128)S(1)} %get-tuple-element.9.refs_1_, f32[16,512]{1,0:T(8,128)S(1)} %get-tuple-element.10.refs_2_, f32[16,128]{1,0:T(8,128)S(1)} %get-tuple-element.11.refs_3_), custom_call_target="tpu_custom_call" | custom-call | bytes 1200000 | tf_op jit(solution)/shard_map/pallas_call | solution.py:838

commit v5 on v4

--- a/solution.py
+++ b/solution.py
@@ -378,7 +378,7 @@
 
     pair_pack.start(sibling)
     each(nc, my, lambda to: pack_copy(to, my).start())
-    for exchange in ex_dy:
+    for exchange in (*ex_dy, ex_x[0]):
         exchange.start_all()
 
     def hand_on(chip):
@@ -393,7 +393,7 @@
         ).start()
 
     each(nc, my, hand_on)
-    for exchange in ex_x:
+    for exchange in ex_x[1:]:
         exchange.start_all()
     pair_pack.arrived()
     relay.arrived()
@@ -480,7 +480,6 @@
         line_in[mx] = product
         if nx > 1:
             ex_line_decay.start_all()
-            ex_line_decay.arrived()
 
     def scan_line(u):
         @pl.when(my_half == u.half)
@@ -607,10 +606,12 @@
     scan_line(grads_a)
     own_x.wait()
     send_state(states_a)
+    send_state(states_b)
+    send_state(states_c)
+    if nx > 1:
+        ex_line_decay.arrived()
     scan_turn(grads_a)
     scan_line(grads_b)
-    send_state(states_b)
-    send_state(states_c)
     lax.fori_loop(pairs // 2, pairs, fill_summed, 0)
     scan_turn(grads_b)
     scan_line(states_a)

time: 71.5 us -> 71.7 us (level)
  no operation moved by 1% of the time
where the time goes in v5:
time: 71.7 us; the launch traced here: 70.8 us
  Pallas kernels  70.2 us (98%)
    pallas_call x1, Pallas kernels, on_device(): pl.pallas_call(functools.partial(kernel, nh, nx, nz, groups), out_shape=(...  69.3 us

profile of v5, /device:TPU:1, one launch (start us, length us, event | category | flops | bytes accessed | tf_op | source)
XLA Modules:
  0.0 70.8 jit_solution(7971300960845629248)
XLA Ops:
  0.6 69.3 %shard_map.102 = (f32[16,8192]{1,0:T(8,128)S(1)}, f32[16,512]{1,0:T(8,128)S(1)}, f32[16,512]{1,0:T(8,128)S(1)}, f32[16,128]{1,0:T(8,128)S(1)}) custom-call(f32[8]{0:T(128)} %rate_hbm.1, f32[8]{0:T(128)} %skip_hbm.1, f32[16,8192]{1,0:T(8,128)} %x_hbm.1, f32[16,8192]{1,0:T(8,128)} %dy_hbm.1, f32[16,512]{1,0:T(8,128)} %write_hbm.1, f32[16,512]{1,0:T(8,128)} %read_hbm.1, ...), custom_call_target="tpu_custom_call" | custom-call | flops 1200000000 | bytes 8000000 | tf_op jit(solution)/shard_map/pallas_call | solution.py:764
  70.0 0.9 %shard_map.103 = (f32[16,8192]{1,0:T(8,128)}, f32[16,512]{1,0:T(8,128)}, f32[16,512]{1,0:T(8,128)}, f32[16,128]{1,0:T(8,128)}) custom-call(f32[16,8192]{1,0:T(8,128)S(1)} %get-tuple-element.8.refs_0_, f32[16,512]{1,0:T(8,128)S(1)} %get-tuple-element.9.refs_1_, f32[16,512]{1,0:T(8,128)S(1)} %get-tuple-element.10.refs_2_, f32[16,128]{1,0:T(8,128)S(1)} %get-tuple-element.11.refs_3_), custom_call_target="tpu_custom_call" | custom-call | bytes 1200000 | tf_op jit(solution)/shard_map/pallas_call | solution.py:839

commit v6 on v5

--- a/solution.py
+++ b/solution.py
@@ -127,7 +127,7 @@
     nh, nx, nz, groups,
     rate_hbm, skip_hbm, x_hbm, dy_hbm, write_hbm, read_hbm, step_hbm,
     dx_ref, dwrite_ref, dread_ref, dstep_ref,
-    rate_ref, skip_ref, write_ref, read_ref, step_ref,
+    rate_ref, skip_ref, write_ref, read_ref, step_ref, x_ref, dy_ref,
     xg, dyg, bg, cg, pack_out, pack_in,
     cum_ref, wide_cum, grow, wide_step, wide_weight,
     decay_top, decay_low, score_top, score_low, grad_top, grad_low, row_sums,
@@ -200,7 +200,9 @@
         along_y, along_z = along_y[2:], along_z[1:]
     if nx > 1:
         each(nx, mx, greet(by_x))
-    for fetch in fetches:
+    fetch_dy = pltpu.make_async_copy(dy_hbm, dy_ref, own_sems.at[8])
+    fetch_x = pltpu.make_async_copy(x_hbm, x_ref, own_sems.at[9])
+    for fetch in (*fetches, fetch_dy, fetch_x):
         fetch.start()
 
     def columns(ref):
@@ -234,7 +236,7 @@
     halves = ((0, part), (part, part))
     ex_dy = [
         along_head(
-            some_columns(dy_hbm, *cut), some_block(dyg, *cut), i, first_rows(dyg, tok, cut)
+            some_columns(dy_ref, *cut), some_block(dyg, *cut), i, first_rows(dyg, tok, cut)
         )
         for i, cut in enumerate(halves)
     ]
@@ -247,7 +249,7 @@
     ]
     ex_x = [
         along_head(
-            some_columns(x_hbm, *cut), some_block(xg, *cut), 4 + i, first_rows(xg, tok, cut)
+            some_columns(x_ref, *cut), some_block(xg, *cut), 4 + i, first_rows(xg, tok, cut)
         )
         for i, cut in enumerate(
             ((0, part), (part, part // 2), (part + part // 2, part // 2))
@@ -356,10 +358,8 @@
             def _(z=2 * i + half):
                 act(z)
 
-    own_dy = pltpu.make_async_copy(columns(dy_hbm)(me), block(dyg, tok)(me), own_sems.at[0])
-    own_x = pltpu.make_async_copy(columns(x_hbm)(me), block(xg, tok)(me), own_sems.at[1])
-    own_dy.start()
-    own_x.start()
+    own_dy = pltpu.make_async_copy(columns(dy_ref)(me), block(dyg, tok)(me), own_sems.at[0])
+    own_x = pltpu.make_async_copy(columns(x_ref)(me), block(xg, tok)(me), own_sems.at[1])
     for fetch in fetches:
         fetch.wait()
     padded = jnp.concatenate([step_ref[...], jnp.zeros((heads - tok, heads), F32)], axis=0)
@@ -374,6 +374,10 @@
         )
     pack_in[me] = pack_out[my]
 
+    fetch_dy.wait()
+    own_dy.start()
+    fetch_x.wait()
+    own_x.start()
     pl.semaphore_wait(barrier, (nh - 1) + (nz - 1) + (nx - 1))
 
     pair_pack.start(sibling)
@@ -777,6 +781,8 @@
             buf(*write_proj.shape),
             buf(*read_proj.shape),
             buf(*step_size.shape),
+            buf(*features.shape),
+            buf(*upstream.shape),
             buf(total, width),
             buf(total, width),
             buf(total, STATE),
@@ -819,7 +825,7 @@
             buf(nc * (tok + hl), STATE),
             pltpu.SemaphoreType.DMA((30, 2)),
             pltpu.SemaphoreType.DMA((1 + nc,)),
-            pltpu.SemaphoreType.DMA((8,)),
+            pltpu.SemaphoreType.DMA((10,)),
         ],
         compiler_params=pltpu.CompilerParams(
             collective_id=0, has_side_effects=True, vmem_limit_bytes=40 * 1024 * 1024

time: 71.7 us -> 71.2 us (level)
  no operation moved by 1% of the time
where the time goes in v6:
time: 71.2 us; the launch traced here: 70.8 us
  Pallas kernels  70.2 us (99%)
    pallas_call x1, Pallas kernels, on_device(): pl.pallas_call(functools.partial(kernel, nh, nx, nz, groups), out_shape=(...  69.3 us

profile of v6, /device:TPU:1, one launch (start us, length us, event | category | flops | bytes accessed | tf_op | source)
XLA Modules:
  0.0 70.8 jit_solution(10775941891906398638)
XLA Ops:
  0.6 69.3 %shard_map.102 = (f32[16,8192]{1,0:T(8,128)S(1)}, f32[16,512]{1,0:T(8,128)S(1)}, f32[16,512]{1,0:T(8,128)S(1)}, f32[16,128]{1,0:T(8,128)S(1)}) custom-call(f32[8]{0:T(128)} %rate_hbm.1, f32[8]{0:T(128)} %skip_hbm.1, f32[16,8192]{1,0:T(8,128)} %x_hbm.1, f32[16,8192]{1,0:T(8,128)} %dy_hbm.1, f32[16,512]{1,0:T(8,128)} %write_hbm.1, f32[16,512]{1,0:T(8,128)} %read_hbm.1, ...), custom_call_target="tpu_custom_call" | custom-call | flops 1200000000 | bytes 8000000 | tf_op jit(solution)/shard_map/pallas_call | solution.py:768
  69.9 0.9 %shard_map.103 = (f32[16,8192]{1,0:T(8,128)}, f32[16,512]{1,0:T(8,128)}, f32[16,512]{1,0:T(8,128)}, f32[16,128]{1,0:T(8,128)}) custom-call(f32[16,8192]{1,0:T(8,128)S(1)} %get-tuple-element.8.refs_0_, f32[16,512]{1,0:T(8,128)S(1)} %get-tuple-element.9.refs_1_, f32[16,512]{1,0:T(8,128)S(1)} %get-tuple-element.10.refs_2_, f32[16,128]{1,0:T(8,128)S(1)} %get-tuple-element.11.refs_3_), custom_call_target="tpu_custom_call" | custom-call | bytes 1200000 | tf_op jit(solution)/shard_map/pallas_call | solution.py:845
